TPU v7x, 32 devices: a whole 2x2x4 slice. The times are simulated.
32 devices in a mesh: dp: 16 (over z, y, core), tensor: 2 (over x).
Axes of the slice: x: 2, y: 2, z: 4, core: 2. Of those that a mesh axis runs over, the one named last changes fastest.
Arguments:
- source: bfloat16 [32, 1024, 512], P('dp', 'tensor'), may hold values from -6 to 6
- target: bfloat16 [32, 1024, 512], P('dp', 'tensor'), may hold values from -6 to 6
- cotangent: bfloat16 [32, 1024, 512], P('dp', 'tensor'), may hold values from -6 to 6
- lengths: int32 [32], P('dp'), may hold values from 128 to 1024, as said below
- timesteps: int32 [32], P('dp'), may hold values from 1 to 50
- masked: int32 [32, 1024], P('dp', 'tensor'), may hold values 0 or 1
- loss_mask: int32 [32, 1024], P('dp', 'tensor'), may hold values 0 or 1
- enc_query: bfloat16 [512, 512], P('dp', 'tensor'), may hold values from -0.25 to 0.25
- enc_key: bfloat16 [512, 512], P('dp', 'tensor'), may hold values from -0.25 to 0.25
- enc_value: bfloat16 [512, 512], P('dp', 'tensor'), may hold values from -0.25 to 0.25
- enc_out: bfloat16 [512, 512], P('tensor', 'dp'), may hold values from -3 to 3
- enc_up: bfloat16 [512, 2048], P('dp', 'tensor'), may hold values from -0.25 to 0.25
- enc_down: bfloat16 [2048, 512], P('tensor', 'dp'), may hold values from -0.125 to 0.125
- self_query: bfloat16 [512, 512], P('dp', 'tensor'), may hold values from -0.25 to 0.25
- self_key: bfloat16 [512, 512], P('dp', 'tensor'), may hold values from -0.25 to 0.25
- self_value: bfloat16 [512, 512], P('dp', 'tensor'), may hold values from -0.25 to 0.25
- self_out: bfloat16 [512, 512], P('tensor', 'dp'), may hold values from -3 to 3
- cross_query: bfloat16 [512, 512], P('dp', 'tensor'), may hold values from -0.25 to 0.25
- cross_key: bfloat16 [512, 512], P('dp', 'tensor'), may hold values from -0.25 to 0.25
- cross_value: bfloat16 [512, 512], P('dp', 'tensor'), may hold values from -0.25 to 0.25
- cross_out: bfloat16 [512, 512], P('tensor', 'dp'), may hold values from -3 to 3
- dec_up: bfloat16 [512, 2048], P('dp', 'tensor'), may hold values from -0.25 to 0.25
- dec_down: bfloat16 [2048, 512], P('tensor', 'dp'), may hold values from -0.125 to 0.125
- norm_gains: float32 [6, 512], replicated, may hold values from 0.1 to 1.9
- norm_shifts: float32 [6, 512], replicated, may hold values from -1.5 to 1.5
- mask_vector: float32 [512], replicated, may hold values from -4 to 4
Outputs:
- decoded: bfloat16 [32, 1024, 512], P('dp', 'tensor')
- source_grad: bfloat16 [32, 1024, 512], P('dp', 'tensor')
- target_grad: bfloat16 [32, 1024, 512], P('dp', 'tensor')
- enc_query_grad: float32 [512, 512], P('dp', 'tensor')
- enc_key_grad: float32 [512, 512], P('dp', 'tensor')
- enc_value_grad: float32 [512, 512], P('dp', 'tensor')
- enc_out_grad: float32 [512, 512], P('tensor', 'dp')
- enc_up_grad: float32 [512, 2048], P('dp', 'tensor')
- enc_down_grad: float32 [2048, 512], P('tensor', 'dp')
- self_query_grad: float32 [512, 512], P('dp', 'tensor')
- self_key_grad: float32 [512, 512], P('dp', 'tensor')
- self_value_grad: float32 [512, 512], P('dp', 'tensor')
- self_out_grad: float32 [512, 512], P('tensor', 'dp')
- cross_query_grad: float32 [512, 512], P('dp', 'tensor')
- cross_key_grad: float32 [512, 512], P('dp', 'tensor')
- cross_value_grad: float32 [512, 512], P('dp', 'tensor')
- cross_out_grad: float32 [512, 512], P('tensor', 'dp')
- dec_up_grad: float32 [512, 2048], P('dp', 'tensor')
- dec_down_grad: float32 [2048, 512], P('tensor', 'dp')
- gains_grad: float32 [6, 512], replicated
- shifts_grad: float32 [6, 512], replicated
- mask_grad: float32 [512], replicated
Inputs may be any that keep to these rules, and one draw needn't show every extreme that they name: `lengths`: among the 2 x 1 pairs of each index of dp one has all 1024 source tokens live.
All inputs are finite; a program needn't handle non-finite values. No bound on the sum of `masked` or of `loss_mask` on one device may be relied on, other than what follows from the above.
Results may differ from a plain program's by a relative error of at most 0.029.
Values may be sent and summed in bfloat16 or wider, within the bound.
A program may use at most 448 MiB of HBM per device.

v0:
```python
import jax
import jax.numpy as jnp
from jax import lax
from jax.experimental import pallas as pl
from jax.experimental.pallas import tpu as pltpu
from jax.sharding import PartitionSpec as P

HD = 64
MICRO = 2
STEPS = 50


eps = 1e-05
floor_score = -1e30


def norm_rows(inputs, gain, shift):
    average = jnp.mean(inputs, axis=-1, keepdims=True)
    centred = inputs - average
    second = jnp.mean(centred * centred, axis=-1, keepdims=True)
    return centred * lax.rsqrt(second + eps) * gain + shift


def norm_back(inputs, gain, shift, gradient):
    unused, pullback = jax.vjp(norm_rows, inputs, gain, shift)
    return pullback(gradient)


def smooth(values):
    return jax.nn.gelu(values, approximate=False)


def spread(inputs):
    return lax.all_gather(inputs.astype(jnp.bfloat16), "tensor", axis=1, tiled=True)


def collect(partial_value):
    return lax.psum_scatter(partial_value, "tensor", scatter_dimension=1, tiled=True)


def spread_grad(gradient):
    return lax.all_gather(gradient.astype(jnp.bfloat16), "tensor", axis=1, tiled=True)


def collect_grad(partial_value):
    return lax.psum_scatter(partial_value, "tensor", scatter_dimension=1, tiled=True)


def project(inputs, weight):
    return jnp.einsum("bsk,kn->bsn", inputs, weight, preferred_element_type=jnp.float32)


def weight_grad(inputs, gradient):
    return jnp.einsum("bsk,bsn->kn", inputs, gradient, preferred_element_type=jnp.float32)


def back_project(gradient, weight):
    return jnp.einsum("bsn,kn->bsk", gradient, weight, preferred_element_type=jnp.float32)


def masked_scores(query_part, key_rows, live):
    scores = jnp.einsum(
        "bqhd,bkhd->bhqk", query_part, key_rows, preferred_element_type=jnp.float32
    ) * HD ** (-0.5)
    return jnp.where(live[:, None, None, :], scores, floor_score)


def attend_forward(query_in, keys_in, w_query, w_key, w_value, live):
    pair_count, length = (query_in.shape[0], query_in.shape[1])
    head_count = w_query.shape[1] // HD
    queries = (
        project(query_in, w_query).astype(jnp.bfloat16).reshape(pair_count, length, head_count, HD)
    )
    key_rows = (
        project(keys_in, w_key).astype(jnp.bfloat16).reshape(pair_count, length, head_count, HD)
    )
    value_rows = (
        project(keys_in, w_value).astype(jnp.bfloat16).reshape(pair_count, length, head_count, HD)
    )
    block_rows = min(512, length)
    pieces = []
    totals = []
    for offset in range(0, length, block_rows):
        scores = masked_scores(queries[:, offset : offset + block_rows], key_rows, live)
        highest = jnp.max(scores, axis=-1, keepdims=True)
        exponent = jnp.exp(scores - highest)
        summed = jnp.sum(exponent, axis=-1, keepdims=True)
        softmax = (exponent / summed).astype(jnp.bfloat16)
        pieces.append(
            jnp.einsum("bhqk,bkhd->bqhd", softmax, value_rows, preferred_element_type=jnp.float32)
        )
        totals.append(highest + jnp.log(summed))
    attended = (
        jnp.concatenate(pieces, axis=1)
        .astype(jnp.bfloat16)
        .reshape(pair_count, length, head_count * HD)
    )
    return (queries, key_rows, value_rows, attended, jnp.concatenate(totals, axis=2))


def attend_backward(whole_grad, query_in, keys_in, w_query, w_key, w_value, w_out, saved, live):
    queries, key_rows, value_rows, attended, totals = saved
    pair_count, length, head_count = (queries.shape[0], queries.shape[1], queries.shape[2])
    scale_score = HD ** (-0.5)
    out_grad = weight_grad(attended, whole_grad)
    head_grad = (
        back_project(whole_grad, w_out)
        .astype(jnp.bfloat16)
        .reshape(pair_count, length, head_count, HD)
    )
    block_rows = min(512, length)
    key_total = jnp.zeros(key_rows.shape, jnp.float32)
    value_total = jnp.zeros(value_rows.shape, jnp.float32)
    query_parts = []
    for offset in range(0, length, block_rows):
        query_part = queries[:, offset : offset + block_rows]
        grad_part = head_grad[:, offset : offset + block_rows]
        scores = masked_scores(query_part, key_rows, live)
        softmax = jnp.exp(scores - totals[:, :, offset : offset + block_rows])
        value_total = value_total + jnp.einsum(
            "bhqk,bqhd->bkhd",
            softmax.astype(jnp.bfloat16),
            grad_part,
            preferred_element_type=jnp.float32,
        )
        soft_grad = jnp.einsum(
            "bqhd,bkhd->bhqk", grad_part, value_rows, preferred_element_type=jnp.float32
        )
        inner = jnp.sum(softmax * soft_grad, axis=-1, keepdims=True)
        score_grad = (softmax * (soft_grad - inner)).astype(jnp.bfloat16)
        query_parts.append(
            jnp.einsum("bhqk,bkhd->bqhd", score_grad, key_rows, preferred_element_type=jnp.float32)
            * scale_score
        )
        key_total = (
            key_total
            + jnp.einsum(
                "bhqk,bqhd->bkhd", score_grad, query_part, preferred_element_type=jnp.float32
            )
            * scale_score
        )
    query_grad = (
        jnp.concatenate(query_parts, axis=1)
        .astype(jnp.bfloat16)
        .reshape(pair_count, length, head_count * HD)
    )
    key_grad = key_total.astype(jnp.bfloat16).reshape(
        pair_count, key_rows.shape[1], head_count * HD
    )
    value_grad = value_total.astype(jnp.bfloat16).reshape(
        pair_count, value_rows.shape[1], head_count * HD
    )
    grads = (
        weight_grad(query_in, query_grad),
        weight_grad(keys_in, key_grad),
        weight_grad(keys_in, value_grad),
        out_grad,
    )
    into_keys = back_project(key_grad, w_key) + back_project(value_grad, w_value)
    return (grads, back_project(query_grad, w_query), into_keys)


def feed_forward(inputs, w_up, w_down):
    lifted = project(inputs, w_up)
    active = smooth(lifted).astype(jnp.bfloat16)
    return (lifted, active, project(active, w_down))


def feed_backward(gradient, inputs, w_up, w_down, lifted, active):
    down_grad = weight_grad(active, gradient)
    active_grad = back_project(gradient, w_down)
    unused, smooth_back = jax.vjp(smooth, lifted)
    lifted_grad = smooth_back(active_grad)[0].astype(jnp.bfloat16)
    return ((weight_grad(inputs, lifted_grad), down_grad), back_project(lifted_grad, w_up))


def body(
    source,
    target,
    cotangent,
    lengths,
    timesteps,
    masked,
    loss_mask,
    enc_query,
    enc_key,
    enc_value,
    enc_out,
    enc_up,
    enc_down,
    self_query,
    self_key,
    self_value,
    self_out,
    cross_query,
    cross_key,
    cross_value,
    cross_out,
    dec_up,
    dec_down,
    norm_gains,
    norm_shifts,
    mask_vector,
):
    pairs_dev, rows_dev = (source.shape[0], source.shape[1])
    per_micro = pairs_dev // MICRO
    seq_len = rows_dev * lax.axis_size("tensor")
    positions = jnp.arange(seq_len)
    gains, shifts = (norm_gains, norm_shifts)
    gain_total = jnp.zeros(norm_gains.shape, jnp.float32)
    shift_total = jnp.zeros(norm_shifts.shape, jnp.float32)
    mask_total = jnp.zeros(mask_vector.shape, jnp.float32)
    decoded_parts = []
    source_parts = []
    target_parts = []
    running = None
    for micro in range(MICRO):
        weights = (
            lax.all_gather(enc_query, "dp", axis=0, tiled=True),
            lax.all_gather(enc_key, "dp", axis=0, tiled=True),
            lax.all_gather(enc_value, "dp", axis=0, tiled=True),
            lax.all_gather(enc_out, "dp", axis=1, tiled=True),
            lax.all_gather(enc_up, "dp", axis=0, tiled=True),
            lax.all_gather(enc_down, "dp", axis=1, tiled=True),
            lax.all_gather(self_query, "dp", axis=0, tiled=True),
            lax.all_gather(self_key, "dp", axis=0, tiled=True),
            lax.all_gather(self_value, "dp", axis=0, tiled=True),
            lax.all_gather(self_out, "dp", axis=1, tiled=True),
            lax.all_gather(cross_query, "dp", axis=0, tiled=True),
            lax.all_gather(cross_key, "dp", axis=0, tiled=True),
            lax.all_gather(cross_value, "dp", axis=0, tiled=True),
            lax.all_gather(cross_out, "dp", axis=1, tiled=True),
            lax.all_gather(dec_up, "dp", axis=0, tiled=True),
            lax.all_gather(dec_down, "dp", axis=1, tiled=True),
        )
        wide = (
            lax.all_gather(weights[4], "tensor", axis=1, tiled=True),
            lax.all_gather(weights[5], "tensor", axis=0, tiled=True),
            lax.all_gather(weights[14], "tensor", axis=1, tiled=True),
            lax.all_gather(weights[15], "tensor", axis=0, tiled=True),
        )
        lower = micro * per_micro
        upper = lower + per_micro
        live = positions[None, :] < lengths[lower:upper][:, None]
        every = jnp.ones((per_micro, seq_len), bool)
        inputs_x = source[lower:upper].astype(jnp.float32)
        rows0 = spread(norm_rows(inputs_x, gains[0], shifts[0]))
        saved0 = attend_forward(rows0, rows0, weights[0], weights[1], weights[2], live)
        stream1 = inputs_x + collect(project(saved0[3], weights[3]))
        normed1 = norm_rows(stream1, gains[1], shifts[1])
        rows1 = normed1.astype(jnp.bfloat16)
        lifted1, active1, partial1 = feed_forward(rows1, wide[0], wide[1])
        stream2 = stream1 + partial1
        memory_rows = spread(norm_rows(stream2, gains[2], shifts[2]))
        chosen = masked[lower:upper][:, :, None] == 1
        start_y = jnp.where(chosen, mask_vector, target[lower:upper].astype(jnp.float32))
        rows3 = spread(norm_rows(start_y, gains[3], shifts[3]))
        saved3 = attend_forward(rows3, rows3, weights[6], weights[7], weights[8], every)
        stream4 = start_y + collect(project(saved3[3], weights[9]))
        rows4 = spread(norm_rows(stream4, gains[4], shifts[4]))
        saved4 = attend_forward(rows4, memory_rows, weights[10], weights[11], weights[12], live)
        stream5 = stream4 + collect(project(saved4[3], weights[13]))
        normed5 = norm_rows(stream5, gains[5], shifts[5])
        rows5 = normed5.astype(jnp.bfloat16)
        lifted5, active5, partial5 = feed_forward(rows5, wide[2], wide[3])
        stream6 = stream5 + partial5
        decoded_parts.append(stream6.astype(jnp.bfloat16))
        factor = (STEPS + 1 - timesteps[lower:upper]).astype(jnp.float32) / STEPS
        grad6 = (
            cotangent[lower:upper].astype(jnp.float32)
            * (factor[:, None] * loss_mask[lower:upper].astype(jnp.float32))[:, :, None]
        )
        (up5, down5), into5 = feed_backward(
            grad6.astype(jnp.bfloat16), rows5, wide[2], wide[3], lifted5, active5
        )
        back5 = norm_back(stream5, gains[5], shifts[5], into5)
        grad5 = grad6 + back5[0]
        grads4, query_term4, memory_term = attend_backward(
            spread_grad(grad5),
            rows4,
            memory_rows,
            weights[10],
            weights[11],
            weights[12],
            weights[13],
            saved4,
            live,
        )
        back4 = norm_back(stream4, gains[4], shifts[4], collect_grad(query_term4))
        grad4 = grad5 + back4[0]
        memory_grad = collect_grad(memory_term)
        grads3, query_term3, keys_term3 = attend_backward(
            spread_grad(grad4),
            rows3,
            rows3,
            weights[6],
            weights[7],
            weights[8],
            weights[9],
            saved3,
            every,
        )
        back3 = norm_back(start_y, gains[3], shifts[3], collect_grad(query_term3 + keys_term3))
        grad_y = grad4 + back3[0]
        target_parts.append(jnp.where(chosen, 0.0, grad_y).astype(jnp.bfloat16))
        mask_total = mask_total + jnp.sum(jnp.where(chosen, grad_y, 0.0), axis=(0, 1))
        back2 = norm_back(stream2, gains[2], shifts[2], memory_grad)
        grad2 = back2[0]
        (up1, down1), into1 = feed_backward(
            grad2.astype(jnp.bfloat16), rows1, wide[0], wide[1], lifted1, active1
        )
        back1 = norm_back(stream1, gains[1], shifts[1], into1)
        grad1 = grad2 + back1[0]
        grads0, query_term0, keys_term0 = attend_backward(
            spread_grad(grad1),
            rows0,
            rows0,
            weights[0],
            weights[1],
            weights[2],
            weights[3],
            saved0,
            live,
        )
        back0 = norm_back(inputs_x, gains[0], shifts[0], collect_grad(query_term0 + keys_term0))
        source_parts.append((grad1 + back0[0]).astype(jnp.bfloat16))
        gain_total = gain_total + jnp.stack(
            [back0[1], back1[1], back2[1], back3[1], back4[1], back5[1]]
        )
        shift_total = shift_total + jnp.stack(
            [back0[2], back1[2], back2[2], back3[2], back4[2], back5[2]]
        )
        up1, down1, up5, down5 = (
            lax.psum_scatter(
                up1.astype(jnp.bfloat16), "tensor", scatter_dimension=1, tiled=True
            ).astype(jnp.float32),
            lax.psum_scatter(
                down1.astype(jnp.bfloat16), "tensor", scatter_dimension=0, tiled=True
            ).astype(jnp.float32),
            lax.psum_scatter(
                up5.astype(jnp.bfloat16), "tensor", scatter_dimension=1, tiled=True
            ).astype(jnp.float32),
            lax.psum_scatter(
                down5.astype(jnp.bfloat16), "tensor", scatter_dimension=0, tiled=True
            ).astype(jnp.float32),
        )
        fresh = (
            grads0[0],
            grads0[1],
            grads0[2],
            grads0[3],
            up1,
            down1,
            grads3[0],
            grads3[1],
            grads3[2],
            grads3[3],
            grads4[0],
            grads4[1],
            grads4[2],
            grads4[3],
            up5,
            down5,
        )
        running = fresh if micro == 0 else jax.tree.map(jnp.add, running, tuple(fresh))
    running = (
        lax.psum_scatter(
            running[0].astype(jnp.bfloat16), "dp", scatter_dimension=0, tiled=True
        ).astype(jnp.float32),
        lax.psum_scatter(
            running[1].astype(jnp.bfloat16), "dp", scatter_dimension=0, tiled=True
        ).astype(jnp.float32),
        lax.psum_scatter(
            running[2].astype(jnp.bfloat16), "dp", scatter_dimension=0, tiled=True
        ).astype(jnp.float32),
        lax.psum_scatter(
            running[3].astype(jnp.bfloat16), "dp", scatter_dimension=1, tiled=True
        ).astype(jnp.float32),
        lax.psum_scatter(
            running[4].astype(jnp.bfloat16), "dp", scatter_dimension=0, tiled=True
        ).astype(jnp.float32),
        lax.psum_scatter(
            running[5].astype(jnp.bfloat16), "dp", scatter_dimension=1, tiled=True
        ).astype(jnp.float32),
        lax.psum_scatter(
            running[6].astype(jnp.bfloat16), "dp", scatter_dimension=0, tiled=True
        ).astype(jnp.float32),
        lax.psum_scatter(
            running[7].astype(jnp.bfloat16), "dp", scatter_dimension=0, tiled=True
        ).astype(jnp.float32),
        lax.psum_scatter(
            running[8].astype(jnp.bfloat16), "dp", scatter_dimension=0, tiled=True
        ).astype(jnp.float32),
        lax.psum_scatter(
            running[9].astype(jnp.bfloat16), "dp", scatter_dimension=1, tiled=True
        ).astype(jnp.float32),
        lax.psum_scatter(
            running[10].astype(jnp.bfloat16), "dp", scatter_dimension=0, tiled=True
        ).astype(jnp.float32),
        lax.psum_scatter(
            running[11].astype(jnp.bfloat16), "dp", scatter_dimension=0, tiled=True
        ).astype(jnp.float32),
        lax.psum_scatter(
            running[12].astype(jnp.bfloat16), "dp", scatter_dimension=0, tiled=True
        ).astype(jnp.float32),
        lax.psum_scatter(
            running[13].astype(jnp.bfloat16), "dp", scatter_dimension=1, tiled=True
        ).astype(jnp.float32),
        lax.psum_scatter(
            running[14].astype(jnp.bfloat16), "dp", scatter_dimension=0, tiled=True
        ).astype(jnp.float32),
        lax.psum_scatter(
            running[15].astype(jnp.bfloat16), "dp", scatter_dimension=1, tiled=True
        ).astype(jnp.float32),
    )
    vectors = lax.psum((gain_total, shift_total, mask_total), ("dp", "tensor"))
    return (
        jnp.concatenate(decoded_parts, axis=0),
        jnp.concatenate(source_parts, axis=0),
        jnp.concatenate(target_parts, axis=0),
        running[0],
        running[1],
        running[2],
        running[3],
        running[4],
        running[5],
        running[6],
        running[7],
        running[8],
        running[9],
        running[10],
        running[11],
        running[12],
        running[13],
        running[14],
        running[15],
        vectors[0],
        vectors[1],
        vectors[2],
    )


F32 = jnp.float32
BF = jnp.bfloat16
LOG2E = 1.4426950408889634
LN2 = 0.6931471805599453
NN = (((1,), (0,)), ((), ()))
NT = (((1,), (1,)), ((), ()))
MESH = pl.DeviceIdType.MESH
RB = 512
FB = 256
VMEM_LIMIT = 63 * 2**20


def dg(left, right, dims=NN):
    return lax.dot_general(left, right, dims, preferred_element_type=F32)


def ln_hat(x):
    centred = x - jnp.mean(x, axis=-1, keepdims=True)
    rstd = lax.rsqrt(jnp.mean(centred * centred, axis=-1, keepdims=True) + eps)
    return centred * rstd, rstd


def ln_back(x, gain, gradient):
    hat, rstd = ln_hat(x)
    scaled = gradient * gain
    first = jnp.mean(scaled, axis=-1, keepdims=True)
    second = jnp.mean(scaled * hat, axis=-1, keepdims=True)
    dx = rstd * (scaled - first - hat * second)
    dgain = jnp.sum(gradient * hat, axis=0, keepdims=True)
    dshift = jnp.sum(gradient, axis=0, keepdims=True)
    return dx, dgain, dshift


def gelu_both(u):
    size = jnp.abs(u)
    t = 1.0 / (1.0 + (0.3275911 * 0.7071067811865476) * size)
    ex = jnp.exp2(u * u * (-0.5 * LOG2E))
    poly = t * (
        0.127414796
        + t * (-0.142248368 + t * (0.7107068705 + t * (-0.7265760135 + t * 0.5307027145)))
    )
    tail = poly * ex
    phi = jnp.where(u > 0, 1.0 - tail, tail)
    return u * phi, phi + u * ex * 0.3989422804014327


def rows_loop(total, step, run):
    def once(i, carry):
        run(pl.ds(pl.multiple_of(i * step, step), step))
        return carry

    lax.fori_loop(0, total // step, once, 0)


def load_weight(w_hbm, offset, width, dst, sems, base):
    copies = []
    for t in range(2):
        src = pl.ds(offset, width)
        to = pl.ds(t * width, width)
        cp = pltpu.make_async_copy(
            w_hbm.at[t, :, src] if len(w_hbm.shape) == 3 else w_hbm.at[t, :, :, :, :, src],
            dst.at[:, to] if len(dst.shape) == 2 else dst.at[:, :, :, :, to],
            sems.at[base + t],
        )
        cp.start()
        copies.append(cp)
    return copies


def wait_all(copies):
    for cp in copies:
        cp.wait()


def columns(ref, lower, width):
    value = ref[..., pl.ds(lower, width)]
    return value if value.ndim == 2 else value.reshape(-1, width)


def whole(ref):
    value = ref[...]
    return value if value.ndim == 2 else value.reshape(-1, value.shape[-1])


def normalize(x, gain, shift, a):
    def run(sl):
        hat, unused = ln_hat(x[sl, :].astype(F32))
        a[sl, :] = (hat * gain + shift).astype(BF)

    rows_loop(x.shape[0], RB, run)


def product_into(a, w, to, scale):
    def run(sl):
        value = dg(a[sl, :], whole(w))
        to[sl, :] = (value if scale is None else value * scale).astype(BF)

    rows_loop(a.shape[0], RB, run)


def attn_project(a, kv, wq, wk, wv, q, k, v):
    product_into(a, wq, q, LOG2E * HD**-0.5)
    product_into(kv, wk, k, None)
    product_into(kv, wv, v, None)


def score_copy(p, h, e_hbm, ebuf, esem):
    slot = lax.rem(p, 2) * 2 + h
    return pltpu.make_async_copy(ebuf.at[slot], e_hbm.at[2 * p + h], esem.at[slot])


def drain_scores(e_hbm, ebuf, esem):
    for p in range(2):
        for h in range(2):
            score_copy(p, h, e_hbm, ebuf, esem).wait()


def attn_core(length, q, k, v, o, ol, r, e_hbm, ebuf, esem, between, fresh):
    seq = q.shape[0]
    pairs = q.shape[1] // 128
    block = 256
    lane = lax.broadcasted_iota(jnp.int32, (1, 128), 1)
    low = lane < 64
    one = jnp.ones((), BF)
    key = lax.broadcasted_iota(jnp.int32, (seq, 1), 0)
    bias = jnp.where(key < length, 0.0, floor_score).astype(F32)
    items = [(b, h) for b in range(seq // block) for h in range(2)]

    def pair(p, carry):
        @pl.when((p > 1) if fresh else (p >= 0))
        def unused_wait():
            score_copy(p, 0, e_hbm, ebuf, esem).wait()
            score_copy(p, 1, e_hbm, ebuf, esem).wait()

        base = lax.rem(p, 2) * 2
        cols = pl.ds(pl.multiple_of(p * 128, 128), 128)
        kp = k[:, cols].astype(F32)
        vp = v[:, cols]
        ka = (
            jnp.where(low, kp, jnp.where(lane == 64, bias, 0.0)).astype(BF),
            jnp.where(low, jnp.where(lane == 0, bias, 0.0), kp).astype(BF),
        )
        va = jnp.where(low, vp, one), jnp.where(low, one, vp)

        def scores(b, h):
            qp = q[pl.ds(b * block, block), cols]
            return dg(jnp.where(low, qp, one) if h == 0 else jnp.where(low, one, qp), ka[h], NT)

        parts = []
        s = scores(*items[0])
        for n, (b, h) in enumerate(items):
            sl = pl.ds(b * block, block)
            following = scores(*items[n + 1]) if n + 1 < len(items) else None
            e = jnp.exp2(s - jnp.max(s, axis=-1, keepdims=True)).astype(BF)
            ebuf[base + h, sl, :] = e
            parts.append(dg(e, va[h]))
            s = following
            if h == 1:
                first, second = parts
                parts = []
                inverse = 1.0 / pltpu.roll(jnp.where(low, second, first), 64, 1)
                r[sl, cols] = inverse.astype(BF)
                joined = jnp.where(low, first, second) * inverse
                rounded = joined.astype(BF)
                o[sl, cols] = rounded
                ol[sl, cols] = (joined - rounded.astype(F32)).astype(BF)
        score_copy(p, 0, e_hbm, ebuf, esem).start()
        score_copy(p, 1, e_hbm, ebuf, esem).start()
        return carry

    lax.fori_loop(0, pairs // 2, pair, 0)
    between()
    lax.fori_loop(pairs // 2, pairs, pair, 0)


def attn_join(x, o, wo, y, lowered):
    def run(sl):
        joined = x[sl, :].astype(F32) + dg(o[sl, :], whole(wo), NT)
        y[sl, :] = joined
        if lowered is not None:
            lowered[sl, :] = joined.astype(BF)

    rows_loop(x.shape[0], RB, run)


def first_scores(e_hbm, ebuf, esem):
    for h in range(2):
        pltpu.make_async_copy(e_hbm.at[h], ebuf.at[h], esem.at[h]).start()


def attn_back_core(q, k, v, do, o, ol, e_hbm, ebuf, esem, ds, dq, dk, dv, between):
    seq = q.shape[0]
    heads = e_hbm.shape[0]
    block = 512
    lane = lax.broadcasted_iota(jnp.int32, (1, 128), 1)
    low = lane < 64
    zero = jnp.zeros((), BF)
    one = jnp.ones((), BF)
    row2 = lax.broadcasted_iota(jnp.int32, (256, 128), 0)
    col2 = lax.broadcasted_iota(jnp.int32, (256, 128), 1)
    swap = jnp.where(((row2 // 64) % 2) != (col2 // 64), 1.0, 0.0).astype(BF)

    def fetch(p, h):
        slot = lax.rem(p, 2) * 2 + h
        return pltpu.make_async_copy(e_hbm.at[2 * p + h], ebuf.at[slot], esem.at[slot])

    def pair(p, carry):
        cols = pl.ds(pl.multiple_of(p * 128, 128), 128)
        fetch(p, 0).wait()
        fetch(p, 1).wait()

        @pl.when(p + 1 < heads // 2)
        def unused_fetch():
            fetch(p + 1, 0).start()
            fetch(p + 1, 1).start()

        base = lax.rem(p, 2) * 2
        qp, kp, vp, dop = q[:, cols], k[:, cols], v[:, cols], do[:, cols]
        product = dop.astype(F32) * (o[:, cols].astype(F32) + ol[:, cols].astype(F32))
        high = product.astype(BF)
        rest = (product - high.astype(F32)).astype(BF)
        inner = -dg(jnp.concatenate([high, rest], axis=1), swap)
        inner_high = inner.astype(BF)
        inner_rest = (inner - inner_high.astype(F32)).astype(BF)
        do_t, q_t = dop.T, qp.T
        lhs = (
            jnp.where(low, dop, jnp.where(lane == 64, inner_high, inner_rest)),
            jnp.where(low, jnp.where(lane == 0, inner_high, inner_rest), dop),
        )
        va = (
            jnp.where(low, vp, jnp.where(lane < 66, one, zero)),
            jnp.where(low, jnp.where(lane < 2, one, zero), vp),
        )
        km = jnp.concatenate([jnp.where(low, kp, zero), jnp.where(low, zero, kp)], axis=0)
        dvs = [dg(do_t, ebuf[base + h])[64 * h : 64 * h + 64] for h in range(2)]
        for h in range(2):
            for b in range(seq // block):
                sl = pl.ds(b * block, block)
                t = dg(lhs[h][b * block : (b + 1) * block], va[h], NT)
                ds[sl, pl.ds(h * seq, seq)] = ebuf[base + h, sl, :] * t.astype(BF)
        dks = [dg(q_t, ds[:, pl.ds(h * seq, seq)])[64 * h : 64 * h + 64] for h in range(2)]
        dq_sum = dg(ds[...], km)
        dq[:, cols] = (dq_sum * HD**-0.5).astype(BF)
        dk[:, cols] = (jnp.concatenate(dks, axis=0) * LN2).astype(BF).T
        dv[:, cols] = jnp.concatenate(dvs, axis=0).astype(BF).T
        return carry

    lax.fori_loop(0, heads // 4, pair, 0)
    between()
    lax.fori_loop(heads // 4, heads // 2, pair, 0)


def places():
    d = lax.axis_index("dp")
    return lax.axis_index("tensor"), d // 4, (d // 2) % 2, d % 2


def at(t, z, y, c):
    return (z * 4 + y * 2 + c, t)


def greet(partners):
    barrier = pltpu.get_barrier_semaphore()
    for device in partners:
        pl.semaphore_signal(barrier, inc=1, device_id=device, device_id_type=MESH)
    pl.semaphore_wait(barrier, len(partners))


def all_partners(t, z, y, c):
    others = [at(t, lax.rem(z + j, 4), y, c) for j in range(1, 4)]
    return [at(t, z, y, 1 - c), at(1 - t, z, y, c), at(t, z, 1 - y, c)] + others


class Saver:
    def __init__(self, sems):
        self.sems, self.count, self.live = sems, 0, []

    def __call__(self, src, dst, slot=None):
        cp = pltpu.make_async_copy(src, dst, self.sems.at[self.count])
        cp.start()
        self.count += 1
        self.live.append((slot, cp))

    def free(self, slot):
        for name, cp in self.live:
            if name == slot:
                cp.wait()
        self.live = [entry for entry in self.live if entry[0] != slot]

    def finish(self):
        for name, cp in self.live:
            cp.wait()
        self.live = []


GATHER_PLAN = (
    ((0, 0), (1, 0), (2, 0), (4, 0), (5, 0), (6, 0)),
    ((0, 1), (1, 1), (3, 0)),
    ((0, 2),),
    ((1, 2), (2, 1), (3, 1)),
    ((7, 0),),
    ((0, 3), (0, 4), (1, 3), (1, 4), (2, 2), (4, 1)),
    (),
    ((3, 2), (5, 1)),
    ((7, 1),),
    ((2, 3), (2, 4)),
    ((4, 2),),
    (),
    ((5, 2), (6, 1), (7, 2)),
    ((3, 3), (4, 3)),
    ((3, 4), (4, 4)),
    ((5, 3),),
    ((5, 4), (6, 2)),
    (),
    (),
    ((6, 3), (7, 3)),
    (),
    ((6, 4), (7, 4)),
)
GATHER_ORDERS = (
    ("zxy",), ("zxy",), ("zxy",), ("xyz",), ("zxy", "zyx"), ("zxy", "zyx"), ("zxy", "zyx"), ("xyz",),
)


class Gather:
    def __init__(self, own, out, send, recv, widths):
        self.own, self.out, self.send, self.recv = own, out, send, recv
        self.starts = [sum(widths[:i]) for i in range(len(widths))]
        self.widths = widths
        self.spot = places()
        self.sends, self.pending = [], {}

    def push(self, src, dst, k, i, device):
        copy = pltpu.make_async_remote_copy(
            src_ref=src, dst_ref=dst, send_sem=self.send.at[k, i], recv_sem=self.recv.at[k, i],
            device_id=device, device_id_type=MESH,
        )
        copy.start()
        self.sends.append(copy)
        self.pending.setdefault(k, []).append(copy)

    def move(self, point):
        for k, s in GATHER_PLAN[point]:
            self.stage(k, s)

    def stage(self, k, s):
        t, z, y, c = self.spot
        every = slice(None)
        for copy in self.pending.pop(k, ()):
            copy.wait_recv()
        if s == 3:
            a = self.out.at[:, :, :, c, :, pl.ds(self.starts[k], self.widths[k])]
            self.push(a, a, k, 10, at(t, z, y, 1 - c))
        if s > 2:
            return
        orders = GATHER_ORDERS[k]
        width = self.widths[k] // len(orders)
        for i, order in enumerate(orders):
            cols = pl.ds(self.starts[k] + i * width, width)
            known = order[:s]
            dst = self.out.at[
                every if "x" in known else t, every if "z" in known else z, every if "y" in known else y, c, :, cols
            ]
            src = self.own.at[:, cols] if s == 0 else dst
            if order[s] == "z":
                for j in range(1, 4):
                    self.push(src, dst, k, 5 * i + j - 1, at(t, lax.rem(z + j, 4), y, c))
            elif order[s] == "x":
                self.push(src, dst, k, 5 * i + 3, at(1 - t, z, y, c))
            else:
                self.push(src, dst, k, 5 * i + 4, at(t, z, 1 - y, c))

    def finish(self):
        for copy in self.sends:
            copy.wait_send()


class Exchange:
    def __init__(self, send, recv, local):
        self.send, self.recv, self.local = send, recv, local
        self.open = []

    def start(self, i, src, kept, dst):
        t, z, y, c = places()
        far = pltpu.make_async_remote_copy(
            src_ref=src, dst_ref=dst, send_sem=self.send.at[i], recv_sem=self.recv.at[i],
            device_id=at(1 - t, z, y, c), device_id_type=MESH,
        )
        near = pltpu.make_async_copy(kept, dst, self.local.at[i])
        far.start()
        near.start()
        self.open.append(far)
        return far, near

    def give(self, i, halves, dst, part=0, parts=1):
        t = lax.axis_index("tensor")
        rows = halves.shape[1]
        take = rows // parts
        mine = dst.at[pl.ds(pl.multiple_of(t * rows + part * take, take), take), :]
        some = pl.ds(part * take, take)
        return self.start(i, halves.at[1 - t, some, :], halves.at[t, some, :], mine)

    def back(self, i, pair, dst):
        t = lax.axis_index("tensor")
        rows = dst.shape[1]
        kept = pair.at[pl.ds(pl.multiple_of(t * rows, rows), rows), :]
        sent = pair.at[pl.ds(pl.multiple_of((1 - t) * rows, rows), rows), :]
        return self.start(i, sent, kept, dst.at[t])

    def finish(self):
        for far in self.open:
            far.wait_send()


def arrived(copies):
    far, near = copies
    near.wait()
    far.wait_recv()


def column(values):
    return jnp.broadcast_to(values, (128, values.shape[1])).T[:, :1]


def weight_loader(w_hbm, sems):
    loads = {}

    def load(name, offset, refs, n, base):
        loads[name] = []
        for i, ref in enumerate(refs):
            loads[name] += load_weight(w_hbm, offset + i * n, n, ref, sems, base + 2 * i)

    def ready(name):
        wait_all(loads[name])

    return load, ready


TURNED = (3, 5, 9, 13, 15)
PACKED = (0, 1, 2, 3, 6, 7, 8, 9, 4, 5, 10, 11, 12, 13, 14, 15)


def forward(
    lengths, timesteps, gains, shifts, mask_row, masked, loss_mask, *refs,
):
    matrices, refs = refs[:16], refs[16:]
    (
        src_hbm, target_hbm, cot_hbm,
        w_hbm, x_o, y0_o, g3_o,
        a0_o, q0_o, k0_o, v0_o, o0_o, ol0_o, r0_o, e0_o, x1_o, a1_o, h1_o, gp1_o, x2_o, mem_o,
        a3_o, q3_o, k3_o, v3_o, o3_o, ol3_o, r3_o, e3_o, y1_o,
        a4_o, q4_o, k4_o, v4_o, o4_o, ol4_o, r4_o, e4_o, y2_o,
        own, tgt, cot, x, y0, wq, wk, wv, wo, sq, sk, sv, so, wu, wd,
        a, q, k, v, o, ol, r, a3, q3, k3, v3, o3, ol3, r3,
        x1, a1, h, gp, x2, mem, y1, y2, ebuf,
        gsend, grecv, xsend, xrecv, local, wsem, esem, osem,
    ) = refs
    t, z, y, c = places()
    seq, width = x.shape
    n1, n2 = width // 2, h.shape[1] // 2
    in_tgt = pltpu.make_async_copy(target_hbm, tgt, local.at[5])
    in_cot = pltpu.make_async_copy(cot_hbm, cot, local.at[6])
    in_tgt.start()
    in_cot.start()
    offset = 0
    for i in PACKED:
        part = matrices[i][...]
        own[:, pl.ds(offset, part.shape[1])] = part
        offset += part.shape[1]
    greet(all_partners(t, z, y, c))
    halves = Exchange(xsend, xrecv, local)
    gather = Gather(own, w_hbm, gsend, grecv, (2 * n1, 2 * n1, 4 * n1, n2, n2, 4 * n1, n2, n2))
    mine = pltpu.make_async_copy(own, w_hbm.at[t, z, y, c], local.at[4])
    mine.start()
    gather.move(0)
    x_in = [halves.give(0, src_hbm, x, 0, 2)]
    save = Saver(osem)
    in_tgt.wait()
    for i in range(2):
        chosen = column(masked[i : i + 1, :].astype(F32)) == 1.0
        tgt[i] = jnp.where(chosen, mask_row[...], tgt[i].astype(F32)).astype(BF)
    mine.wait()
    gather.move(1)
    in_cot.wait()
    for i in range(2):
        factor = (STEPS + 1 - timesteps[i]).astype(F32) / STEPS
        weight = column(loss_mask[i : i + 1, :].astype(F32)) * factor
        cot[i] = (cot[i].astype(F32) * weight).astype(BF)
    gather.move(2)
    x_in.append(halves.give(3, src_hbm, x, 1, 2))
    gather.move(3)
    for copies in x_in:
        arrived(copies)
    normalize(x, gains[0:1, :], shifts[0:1, :], a)
    save(x, x_o, "x")
    save(a, a0_o, "A")
    gather.move(4)
    gather.move(5)
    load, ready = weight_loader(w_hbm, wsem)
    load("enc", 0, (wq, wk), n1, 0)
    load("out", 2 * n1, (wv, wo), n1, 4)
    ready("enc")
    product_into(a, wq, q, LOG2E * HD**-0.5)
    product_into(a, wk, k, None)
    gather.move(6)
    y0_in = halves.give(1, tgt, y0)
    ready("out")
    product_into(a, wv, v, None)
    for src, dst in ((q, q0_o), (k, k0_o), (v, v0_o)):
        save(src, dst, "A")
    gather.move(7)
    length = lengths[t]

    def between0():
        gather.move(8)

    attn_core(length, q, k, v, o, ol, r, e0_o, ebuf, esem, between0, True)
    gather.move(9)
    load("self", 4 * n1, (sq, sk, sv, so), n1, 8)
    for src, dst in ((o, o0_o), (ol, ol0_o), (r, r0_o)):
        save(src, dst, "A")
    arrived(y0_in)
    save(y0, y0_o, "y0")
    normalize(y0, gains[3:4, :], shifts[3:4, :], a3)
    gather.move(10)
    save.free("x")
    attn_join(x, o, wo, x1, x)
    save(x, x1_o)
    ready("self")
    attn_project(a3, a3, sq, sk, sv, q3, k3, v3)
    for src, dst in ((a3, a3_o), (q3, q3_o), (k3, k3_o), (v3, v3_o)):
        save(src, dst)
    gather.move(11)
    gather.move(12)
    g3_in = halves.give(2, cot, g3_o)

    def between3():
        gather.move(13)

    attn_core(seq, q3, k3, v3, o3, ol3, r3, e3_o, ebuf, esem, between3, False)
    gather.move(14)
    load("feed", 8 * n1, (wu, wd), n2, 16)
    for src, dst in ((o3, o3_o), (ol3, ol3_o), (r3, r3_o)):
        save(src, dst)
    save.free("y0")
    attn_join(y0, o3, so, y1, y0)
    save(y0, y1_o)
    save.free("A")
    normalize(y1, gains[4:5, :], shifts[4:5, :], a)
    gather.move(15)
    ready("feed")

    def feed(sl):
        stream = x1[sl, :]
        hat, unused = ln_hat(stream)
        rows = (hat * gains[1:2, :] + shifts[1:2, :]).astype(BF)
        a1[sl, :] = rows
        out = stream
        lifted = dg(rows, columns(wu, 0, FB))
        for lower in range(0, 2 * n2, FB):
            cols = pl.ds(lower, FB)
            following = dg(rows, columns(wu, lower + FB, FB)) if lower + FB < 2 * n2 else None
            active, slope = gelu_both(lifted)
            active = active.astype(BF)
            h[sl, cols] = active
            gp[sl, cols] = slope.astype(BF)
            out = out + dg(active, columns(wd, lower, FB), NT)
            lifted = following
        x2[sl, :] = out.astype(BF)
        hat, unused = ln_hat(out)
        mem[sl, :] = (hat * gains[2:3, :] + shifts[2:3, :]).astype(BF)

    rows_loop(seq // 2, RB, feed)
    gather.move(16)
    load("cross", 8 * n1 + 2 * n2, (wq, wk, wv, wo), n1, 0)
    rows_loop(seq // 2, RB, lambda sl: feed(pl.ds(pl.multiple_of(seq // 2 + sl.start, RB), RB)))
    for src, dst in ((a1, a1_o), (h, h1_o), (gp, gp1_o), (x2, x2_o), (mem, mem_o)):
        save(src, dst)
    gather.move(17)
    ready("cross")
    attn_project(a, mem, wq, wk, wv, q, k, v)
    for src, dst in ((a, a4_o), (q, q4_o), (k, k4_o), (v, v4_o)):
        save(src, dst)
    gather.move(18)

    def between4():
        gather.move(19)

    attn_core(length, q, k, v, o, ol, r, e4_o, ebuf, esem, between4, False)
    for src, dst in ((o, o4_o), (ol, ol4_o), (r, r4_o)):
        save(src, dst)
    gather.move(20)
    attn_join(y1, o, wo, y2, None)
    save(y2, y2_o)
    gather.move(21)
    drain_scores(e4_o, ebuf, esem)
    arrived(g3_in)
    halves.finish()
    gather.finish()
    save.finish()


class Reduce:
    def __init__(self, out, chunks):
        self.out, self.chunks = out, chunks
        self.spot = places()
        self.sends, self.pending = [], {}

    def push(self, name, i, src, dst, device):
        send, recv = self.chunks[name][5:7]
        copy = pltpu.make_async_remote_copy(
            src_ref=src, dst_ref=dst, send_sem=send.at[i], recv_sem=recv.at[i],
            device_id=device, device_id_type=MESH,
        )
        copy.start()
        self.sends.append((name, copy))
        self.pending.setdefault(name, []).append(copy)

    def move(self, *steps):
        for name, s in steps:
            self.stage(name, s)

    def stage(self, name, s):
        t, z, y, c = self.spot
        g, r1, r2, r3, r4, send, recv, start, split = self.chunks[name]
        width = g.shape[-1]
        half = width // 2 if split else width
        left = pl.ds(0, half)
        right = pl.ds(half, half)
        by_x, by_y = at(1 - t, z, y, c), at(t, z, 1 - y, c)

        def add(mine, theirs):
            mine[...] = (mine[...].astype(F32) + theirs[...].astype(F32)).astype(BF)

        for copy in self.pending.pop(name, ()):
            copy.wait_recv()
        if s == 0:
            self.push(name, 0, g.at[:, :, :, 1 - c], r1, at(t, z, y, 1 - c))
        elif s == 1:
            add(g.at[:, :, 1 - y, c], r1.at[:, :, 1 - y])
            self.push(name, 1, g.at[:, :, 1 - y, c, :, left], r2.at[:, :, :, left], by_y)
            add(g.at[:, :, y, c], r1.at[:, :, y])
            if split:
                self.push(name, 2, g.at[1 - t, :, :, c, :, right], r3.at[0], by_x)
        elif s == 2:
            rows = g.at[:, :, y, c, :, left]
            add(rows, r2.at[:, :, :, left])
            if not split:
                self.push(name, 2, g.at[1 - t, :, y, c], r3, by_x)
            else:
                self.push(name, 3, g.at[1 - t, :, y, c, :, left], r3.at[1, :, 0], by_x)
                add(g.at[t, :, :, c, :, right], r3.at[0])
                self.push(name, 4, g.at[t, :, 1 - y, c, :, right], r3.at[1, :, 1], by_y)
        elif s == 3:
            if not split:
                add(g.at[t, :, y, c], r3)
            else:
                add(g.at[t, :, y, c, :, left], r3.at[1, :, 0])
                add(g.at[t, :, y, c, :, right], r3.at[1, :, 1])
            for j in range(1, 4):
                zz = lax.rem(z + j, 4)
                self.push(name, 4 + j, g.at[t, zz, y, c], r4.at[j - 1], at(t, zz, y, c))
        elif s == 4:
            self.out[:, pl.ds(start, width)] = (g[t, z, y, c].astype(F32) + r4[0].astype(F32)) + (
                r4[1].astype(F32) + r4[2].astype(F32)
            )

    def release(self, name):
        for owner, copy in self.sends:
            if owner == name:
                copy.wait_send()
        self.sends = [entry for entry in self.sends if entry[0] != name]

    def finish(self):
        for owner, copy in self.sends:
            copy.wait_send()
        self.sends = []


def put(g, first, n, value, lower=0):
    done = 0
    while done < value.shape[1]:
        t, offset = (lower + done) // n, (lower + done) % n
        take = min(value.shape[1] - done, n - offset)
        block = value[:, done : done + take].astype(BF)
        g[t, :, :, :, :, pl.ds(first + offset, take)] = block.reshape(g.shape[1:5] + (take,))
        done += take


def add_norm(ng, index, dgain, dshift):
    ng[index : index + 1, :] += dgain
    ng[6 + index : 7 + index, :] += dshift


def attn_backward(
    g, x, gain, ng, index, a_t, kv_t, g_t, wq, wk, wv, wo, q, k, v, o, ol, r, e_hbm, ebuf, esem, ds,
    do, dq, dk, dv, grads, n1, before_core, between, after_core, after_grads, into_keys, finish,
):
    seq = x.shape[0]

    def before(sl):
        rows = g[sl, :].astype(BF)
        g_t[:, sl] = rows.T
        do[sl, :] = (dg(rows, wo[...]) * r[sl, :].astype(F32)).astype(BF)

    rows_loop(seq, RB, before)
    put(grads, 3 * n1, n1, dg(g_t[...], o[...]))
    before_core()
    attn_back_core(q, k, v, do, o, ol, e_hbm, ebuf, esem, ds, dq, dk, dv, between)
    after_core()
    put(grads, 0, n1, dg(a_t[...], dq[...]))
    put(grads, n1, n1, dg(kv_t[...], dk[...]))
    put(grads, 2 * n1, n1, dg(kv_t[...], dv[...]))
    after_grads()

    def after(sl):
        into = dg(dq[sl, :], wq[...], NT)
        keys = dg(dk[sl, :], wk[...], NT) + dg(dv[sl, :], wv[...], NT)
        if into_keys is None:
            into = into + keys
        else:
            into_keys[sl, :] = keys
        dx, dgain, dshift = ln_back(x[sl, :].astype(F32), gain, into)
        add_norm(ng, index, dgain, dshift)
        finish(sl, g[sl, :] + dx)

    rows_loop(seq, RB, after)


def fetcher(sems):
    count = [0]

    def fetch(*pairs):
        copies = []
        for src, dst in pairs:
            cp = pltpu.make_async_copy(src, dst, sems.at[count[0]])
            count[0] += 1
            cp.start()
            copies.append(cp)
        return copies

    return fetch


def nothing():
    return None


def dec_backward(
    gains, shifts, y2_hbm, g3_hbm, y1_hbm, mem_hbm, a4_hbm, q4_hbm, k4_hbm, v4_hbm, o4_hbm, ol4_hbm, r4_hbm, e4_hbm,
    x2_hbm, x1_hbm, a1_hbm, h1_hbm, gp1_hbm, w_hbm,
    dec_o, g4_o, g1_o, up_o, down_o, sums, ng,
    y2, g3, y1, a, q, k, v, o, ol, r, cq, ck, cv, co, wu, wd,
    big, gs, do, a_t, g_t, g_up, g_down, g_cross, ebuf,
    ru1, ru2, ru3, ru4, rd1, rd2, rd3, rd4, rc1, rc2, rc3, rc4,
    rsend, rrecv, xsend, xrecv, local, isem, wsem, esem, osem,
):
    t, z, y, c = places()
    seq, width = y1.shape
    n1, n2 = cq.shape[1] // 2, wu.shape[1] // 2
    fetch = fetcher(isem)
    load, ready = weight_loader(w_hbm, wsem)
    first = fetch((y2_hbm, y2), (g3_hbm, g3))
    load("feed", 12 * n1 + 2 * n2, (wu, wd), n2, 0)
    greet(all_partners(t, z, y, c))
    halves = Exchange(xsend, xrecv, local)
    reduce = Reduce(
        sums,
        {
            "up": (g_up, ru1, ru2, ru3, ru4, rsend.at[0], rrecv.at[0], 0, True),
            "down": (g_down, rd1, rd2, rd3, rd4, rsend.at[1], rrecv.at[1], n2, True),
            "cross": (g_cross, rc1, rc2, rc3, rc4, rsend.at[2], rrecv.at[2], 2 * n2, True),
        },
    )
    ng[...] = jnp.zeros_like(ng)
    save = Saver(osem)
    wait_all(first)
    ready("feed")
    load("cross", 8 * n1 + 2 * n2, (cq, ck, cv, co), n1, 4)
    cross = fetch(
        (o4_hbm, o), (r4_hbm, r), (a4_hbm, a), (q4_hbm, q), (k4_hbm, k),
        (v4_hbm, v), (ol4_hbm, ol), (y1_hbm, y1),
    )
    first_scores(e4_hbm, ebuf, esem)
    h, du = big.at[0], big.at[1]

    def feed(sl):
        stream = y2[sl, :]
        hat, unused = ln_hat(stream)
        rows = (hat * gains[5:6, :] + shifts[5:6, :]).astype(BF)
        a_t[:, sl] = rows.T
        grad = g3[sl, :]
        g_t[:, sl] = grad.T
        out, into = stream, None
        lifted, pulled = dg(rows, columns(wu, 0, FB)), dg(grad, columns(wd, 0, FB))
        for lower in range(0, 2 * n2, FB):
            cols = pl.ds(lower, FB)
            if lower + FB < 2 * n2:
                following = dg(rows, columns(wu, lower + FB, FB)), dg(grad, columns(wd, lower + FB, FB))
            active, slope = gelu_both(lifted)
            active = active.astype(BF)
            h[sl, cols] = active
            pushed = (pulled * slope).astype(BF)
            du[sl, cols] = pushed
            out = out + dg(active, columns(wd, lower, FB), NT)
            part = dg(pushed, columns(wu, lower, FB), NT)
            into = part if into is None else into + part
            lifted, pulled = following
        g3[sl, :] = out.astype(BF)
        dx, dgain, dshift = ln_back(stream, gains[5:6, :], into)
        add_norm(ng, 5, dgain, dshift)
        gs[sl, :] = grad.astype(F32) + dx

    rows_loop(seq, RB, feed)
    dec_back = halves.back(0, g3, dec_o)
    block = width
    for j in range(2 * n2 // block):
        put(g_up, 0, n2, dg(a_t[...], du[:, pl.ds(j * block, block)]), j * block)
    reduce.move(("up", 0))
    for j in range(2 * n2 // block):
        put(g_down, 0, n2, dg(g_t[...], h[:, pl.ds(j * block, block)]), j * block)
    load("enc", 8 * n1, (wu, wd), n2, 12)
    reduce.move(("down", 0))
    wait_all(cross)
    ready("cross")
    a_t[...] = a[...].T
    memory = big.at[1, :, pl.ds(3 * width, width)]
    late = fetch((mem_hbm, memory))
    dq, dk, dv = (big.at[1, :, pl.ds(i * width, width)] for i in range(3))

    def before_core():
        reduce.move(("up", 1))

    def between():
        reduce.move(("down", 1))

    def after_core():
        wait_all(late)
        late.clear()
        late.extend(fetch((x2_hbm, r)))
        g_t[...] = memory[...].T
        late.extend(
            fetch(
                (gp1_hbm.at[:, pl.ds(0, n2)], ebuf.at[2]), (gp1_hbm.at[:, pl.ds(n2, n2)], ebuf.at[3]),
                (h1_hbm.at[:, pl.ds(0, n2)], ebuf.at[0]), (h1_hbm.at[:, pl.ds(n2, n2)], ebuf.at[1]),
            )
        )
        reduce.move(("up", 2))

    def after_grads():
        late.extend(fetch((a1_hbm, a)))
        reduce.move(("cross", 0), ("down", 2))

    def keep(sl, gradient):
        gs[sl, :] = gradient

    attn_backward(
        gs, y1, gains[4:5, :], ng, 4, a_t, g_t, g_t, cq, ck, cv, co, q, k, v, o, ol, r, e4_hbm,
        ebuf, esem, big.at[0], do, dq, dk, dv, g_cross, n1,
        before_core, between, after_core, after_grads, y2, keep,
    )
    save(gs, g4_o)
    late.extend(fetch((x1_hbm, y1)))
    reduce.move(("up", 3), ("cross", 1))
    wait_all(late)
    ready("enc")
    save.finish()

    def feed_back(sl):
        dx, dgain, dshift = ln_back(r[sl, :].astype(F32), gains[2:3, :], y2[sl, :])
        add_norm(ng, 2, dgain, dshift)
        grad = dx.astype(BF)
        g_t[:, sl] = grad.T
        a_t[:, sl] = a[sl, :].T
        into = None
        pulled = dg(grad, columns(wd, 0, FB))
        for lower in range(0, 2 * n2, FB):
            i, cols = lower // n2, pl.ds(lower % n2, FB)
            following = dg(grad, columns(wd, lower + FB, FB)) if lower + FB < 2 * n2 else None
            pushed = (pulled * ebuf[2 + i, sl, cols].astype(F32)).astype(BF)
            ebuf[2 + i, sl, cols] = pushed
            part = dg(pushed, columns(wu, lower, FB), NT)
            into = part if into is None else into + part
            pulled = following
        dx1, dgain, dshift = ln_back(y1[sl, :].astype(F32), gains[1:2, :], into)
        add_norm(ng, 1, dgain, dshift)
        gs[sl, :] = dx + dx1

    rows_loop(seq // 2, RB, feed_back)
    reduce.move(("down", 3))
    rows_loop(seq // 2, RB, lambda sl: feed_back(pl.ds(pl.multiple_of(seq // 2 + sl.start, RB), RB)))
    save(gs, g1_o)
    reduce.move(("cross", 2), ("up", 4))
    reduce.release("up")
    for i in range(2):
        for j in range(n2 // block):
            cols = pl.ds(j * block, block)
            put(g_up, 0, n2, dg(a_t[...], ebuf[2 + i, :, cols]), i * n2 + j * block)
    save(g_up, up_o)
    reduce.move(("cross", 3), ("down", 4))
    reduce.release("down")
    for i in range(2):
        for j in range(n2 // block):
            cols = pl.ds(j * block, block)
            put(g_down, 0, n2, dg(g_t[...], ebuf[i, :, cols]), i * n2 + j * block)
    save(g_down, down_o)
    reduce.move(("cross", 4))
    arrived(dec_back)
    halves.finish()
    reduce.finish()
    save.finish()


def last_backward(
    gains, ng2, masked, g4_hbm, g1_hbm, y0_hbm, a3_hbm, q3_hbm, k3_hbm, v3_hbm, o3_hbm, ol3_hbm, r3_hbm, e3_hbm,
    x_hbm, a0_hbm, q0_hbm, k0_hbm, v0_hbm, o0_hbm, ol0_hbm, r0_hbm, e0_hbm, up_hbm, down_hbm, w_hbm,
    sg_o, target_o, sums, vec,
    gs, gs1, x, x0, a, q, k, v, o, ol, r, wq, wk, wv, wo, vo, big, do, a_t, g_t, gy, ng,
    g_up, g_down, g_self, g_enc, ebuf,
    ru1, ru2, ru3, ru4, rd1, rd2, rd3, rd4, rs1, rs2, rs3, rs4, re1, re2, re3, re4, ro1, ro2, ro3, ro4, v1, vr,
    rsend, rrecv, xsend, xrecv, local, vsend, vrecv, isem, wsem, esem,
):
    t, z, y, c = places()
    seq, width = x.shape
    n1 = wq.shape[1] // 2
    n2 = g_up.shape[-1]
    fetch = fetcher(isem)
    load, ready = weight_loader(w_hbm, wsem)
    load("self out", 7 * n1, (wo,), n1, 0)
    first = fetch((g4_hbm, gs), (o3_hbm, o), (r3_hbm, r))
    ups = fetch((up_hbm, g_up), (down_hbm, g_down))
    first_scores(e3_hbm, ebuf, esem)
    second = fetch((q3_hbm, q), (k3_hbm, k), (v3_hbm, v), (ol3_hbm, ol), (a3_hbm, a), (y0_hbm, x))
    load("self", 4 * n1, (wq, wk, wv), n1, 2)
    load("enc out", 3 * n1, (vo,), n1, 8)
    late = fetch((g1_hbm, gs1), (x_hbm, x0))
    greet(all_partners(t, z, y, c))
    halves = Exchange(xsend, xrecv, local)
    reduce = Reduce(
        sums,
        {
            "up": (g_up, ru1, ru2, ru3, ru4, rsend.at[0], rrecv.at[0], 0, True),
            "down": (g_down, rd1, rd2, rd3, rd4, rsend.at[1], rrecv.at[1], n2, True),
            "self": (g_self, rs1, rs2, rs3, rs4, rsend.at[2], rrecv.at[2], 2 * n2, True),
            "enc": (
                g_enc.at[:, :, :, :, :, pl.ds(0, 3 * n1)], re1, re2, re3, re4, rsend.at[3], rrecv.at[3],
                2 * n2 + 4 * n1, True,
            ),
            "out": (
                g_enc.at[:, :, :, :, :, pl.ds(3 * n1, n1)], ro1, ro2, ro3, ro4, rsend.at[4], rrecv.at[4],
                2 * n2 + 7 * n1, False,
            ),
        },
    )
    ng[...] = ng2[...]
    wait_all(ups)
    reduce.move(("up", 0), ("down", 0))
    wait_all(first)
    ready("self out")
    dq, dk, dv = (big.at[1, :, pl.ds(i * width, width)] for i in range(3))
    ds = big.at[0]

    def before_core3():
        wait_all(second)
        a_t[...] = a[...].T
        ready("self")

    def between3():
        reduce.move(("up", 1), ("down", 1))

    def after_core3():
        late.extend(fetch((o0_hbm, o), (r0_hbm, r), (q0_hbm, q), (k0_hbm, k), (v0_hbm, v), (ol0_hbm, ol), (a0_hbm, a)))
        first_scores(e0_hbm, ebuf, esem)

    def after_grads3():
        reduce.move(("self", 0), ("up", 2))

    def last3(sl, gradient):
        gy[sl, :] = gradient.astype(BF)

    attn_backward(
        gs, x, gains[3:4, :], ng, 3, a_t, a_t, g_t, wq, wk, wv, wo, q, k, v, o, ol, r, e3_hbm,
        ebuf, esem, ds, do, dq, dk, dv, g_self, n1,
        before_core3, between3, after_core3, after_grads3, None, last3,
    )
    load("enc", 0, (wq, wk, wv), n1, 10)
    reduce.move(("down", 2), ("self", 1))
    gy_back = halves.back(0, gy, target_o)
    wait_all(late)
    ready("enc out")
    a_t[...] = a[...].T

    def before_core0():
        reduce.move(("out", 0), ("up", 3))

    def between0():
        reduce.move(("out", 1))

    def after_core0():
        reduce.move(("out", 2), ("self", 2), ("down", 3), ("up", 4))
        arrived(gy_back)
        total = jnp.zeros((1, width), F32)
        for i in range(2):
            chosen = column(masked[i : i + 1, :].astype(F32)) == 1.0
            rows = target_o[i].astype(F32)
            total = total + jnp.sum(jnp.where(chosen, rows, 0.0), axis=0, keepdims=True)
            target_o[i] = jnp.where(chosen, 0.0, rows).astype(BF)
        ng[12:13, :] = total

    def after_grads0():
        ready("enc")
        gy_back[0].wait_send()
        reduce.move(("enc", 0))

    def last0(sl, gradient):
        gy[sl, :] = gradient.astype(BF)

    attn_backward(
        gs1, x0, gains[0:1, :], ng, 0, a_t, a_t, g_t, wq, wk, wv, vo, q, k, v, o, ol, r, e0_hbm,
        ebuf, esem, ds, do, dq, dk, dv, g_enc, n1,
        before_core0, between0, after_core0, after_grads0, None, last0,
    )
    waiting = []

    def vector(s):
        for copy in waiting:
            copy.wait_recv()
        waiting.clear()
        if s == 0:
            v1[0] = ng[...]
        elif s < 4:
            v1[s] = v1[s - 1] + vr[s - 1]
        if s < 3:
            targets = ((s, (at(1 - t, z, y, c), at(t, z, y, 1 - c), at(t, z, 1 - y, c))[s]),)
        elif s == 3:
            targets = tuple((2 + j, at(t, lax.rem(z + j, 4), y, c)) for j in range(1, 4))
        else:
            targets = ()
            vec[...] = (v1[3] + vr[3]) + (vr[4] + vr[5])
        for slot, device in targets:
            copy = pltpu.make_async_remote_copy(
                src_ref=v1.at[s], dst_ref=vr.at[slot], send_sem=vsend.at[slot], recv_sem=vrecv.at[slot],
                device_id=device, device_id_type=MESH,
            )
            copy.start()
            reduce.sends.append(("vector", copy))
            waiting.append(copy)

    vector(0)
    reduce.move(("enc", 1), ("self", 3), ("out", 3))
    vector(1)
    reduce.move(("enc", 2))
    sg_back = halves.back(1, gy, sg_o)
    vector(2)
    vector(3)
    reduce.move(("down", 4), ("enc", 3))
    vector(4)
    reduce.move(("self", 4), ("out", 4), ("enc", 4))
    arrived(sg_back)
    sg_back[0].wait_send()
    reduce.finish()


def unpack(sums2, sums3, vec, *refs):
    grads, (gains_o, shifts_o, mask_o) = refs[:16], refs[16:]
    for summed, held in ((sums2, (14, 15, 10, 11, 12, 13)), (sums3, (4, 5, 6, 7, 8, 9, 0, 1, 2, 3))):
        offset = 0
        for i in held:
            n = grads[i].shape[1]
            grads[i][...] = summed[:, pl.ds(offset, n)]
            offset += n
    gains_o[...] = vec[0:6, :]
    shifts_o[...] = vec[6:12, :]
    mask_o[...] = vec[12:13, :]


def compute_all(lengths, timesteps, gains, shifts, mask_vector, masked, loss_mask, matrices, source, target, cotangent):
    rows, width = source.shape[1:]
    seq = 2 * rows
    n1 = width // 2
    part = matrices[0].shape[0]
    n2 = matrices[4].shape[1]
    total = 12 * n1 + 4 * n2
    hidden = 2 * n2
    heads = width // HD
    sd = jax.ShapeDtypeStruct
    any_spec = pl.BlockSpec(memory_space=pl.ANY)
    vmem = pl.BlockSpec(memory_space=pltpu.VMEM)
    smem = pl.BlockSpec(memory_space=pltpu.SMEM)
    dma = pltpu.SemaphoreType.DMA
    row = lambda kind: sd((seq, width), kind)
    tall = lambda kind: sd((seq, hidden), kind)
    halves = sd((2, rows, width), BF)
    escores = sd((heads, seq, seq), BF)
    vrow = lambda kind: pltpu.VMEM((seq, width), kind)
    vhalves = pltpu.VMEM((2, rows, width), BF)
    vsq = pltpu.VMEM((width, width), BF)
    vwide = pltpu.VMEM((width, hidden), BF)
    vtall = pltpu.VMEM((seq, hidden), BF)
    vsq5 = pltpu.VMEM((4, 2, 2, part, width), BF)
    vwide5 = pltpu.VMEM((4, 2, 2, part, hidden), BF)
    turned = pltpu.VMEM((width, seq), BF)
    big = pltpu.VMEM((2, seq, hidden), BF)
    ebuf = pltpu.VMEM((4, seq, seq), BF)
    grads = lambda n: pltpu.VMEM((2, 4, 2, 2, part, n), BF)

    def landing(n, split=False):
        r3 = (2, 4, 2, part, n // 2) if split else (4, part, n)
        return [
            pltpu.VMEM(dims, BF) for dims in ((2, 4, 2, part, n), (2, 4, part, n), r3, (3, part, n))
        ]

    def params(number):
        return pltpu.CompilerParams(
            vmem_limit_bytes=VMEM_LIMIT, collective_id=number, has_side_effects=True
        )

    attention = [row(BF)] * 7 + [escores]
    (
        gathered, x, y0, g3,
        a0, q0, k0, v0, o0, ol0, r0, e0, x1, a1, h1, gp1, x2, mem,
        a3, q3, k3, v3, o3, ol3, r3, e3, y1,
        a4, q4, k4, v4, o4, ol4, r4, e4, y2,
    ) = pl.pallas_call(
        forward,
        in_specs=[smem, smem] + [vmem] * 21 + [any_spec] * 3,
        out_specs=[any_spec] * 36,
        out_shape=[sd((2, 4, 2, 2, part, total), BF)] + [row(BF)] * 3
        + attention + [row(BF), row(BF), tall(BF), tall(BF), row(BF), row(BF)]
        + attention + [row(BF)]
        + attention + [row(F32)],
        scratch_shapes=[pltpu.VMEM((part, total), BF), vhalves, vhalves]
        + [vrow(BF)] * 2 + [vsq5] * 8 + [vwide5] * 2 + [vrow(BF)] * 14
        + [vrow(F32), vrow(BF), vtall, vtall, vrow(BF), vrow(BF), vrow(F32), vrow(F32), ebuf]
        + [dma((8, 11)), dma((8, 11)), dma((4,)), dma((4,)), dma((7,)), dma((20,)), dma((4,)), dma((35,))],
        compiler_params=params(0),
        name="forward",
    )(lengths, timesteps, gains, shifts, mask_vector[None], masked, loss_mask, *matrices, source, target, cotangent)
    weights = gathered.reshape(2, width, total)
    decoded, g4, g1, up, down, sums2, ng = pl.pallas_call(
        dec_backward,
        in_specs=[vmem, vmem] + [any_spec] * 18,
        out_specs=[any_spec] * 5 + [vmem] * 2,
        out_shape=[halves, row(F32), row(F32)] + [sd((2, 4, 2, 2, part, n2), BF)] * 2
        + [sd((part, 2 * n2 + 4 * n1), F32), sd((16, width), F32)],
        scratch_shapes=[vrow(F32)] + [vrow(BF)] * 9
        + [vsq] * 4 + [vwide] * 2 + [big, vrow(F32), vrow(BF)] + [turned] * 2
        + [grads(n2), grads(n2), grads(4 * n1), ebuf]
        + landing(n2, True) + landing(n2, True) + landing(4 * n1, True)
        + [dma((3, 8)), dma((3, 8)), dma((1,)), dma((1,)), dma((1,)), dma((18,)), dma((16,)), dma((4,)), dma((4,))],
        compiler_params=params(1),
        name="dec_backward",
    )(gains, shifts, y2, g3, y1, mem, a4, q4, k4, v4, o4, ol4, r4, e4, x2, x1, a1, h1, gp1, weights)
    source_grad, target_grad, sums3, vec = pl.pallas_call(
        last_backward,
        in_specs=[vmem] * 3 + [any_spec] * 23,
        out_specs=[any_spec, vmem, vmem, vmem],
        out_shape=[halves, halves, sd((part, 2 * n2 + 8 * n1), F32), sd((16, width), F32)],
        scratch_shapes=[vrow(F32)] * 2 + [vrow(BF)] * 9 + [vsq] * 5 + [big, vrow(BF)] + [turned] * 2
        + [vrow(BF), pltpu.VMEM((16, width), F32)]
        + [grads(n2), grads(n2), grads(4 * n1), grads(4 * n1), ebuf]
        + landing(n2, True) + landing(n2, True) + landing(4 * n1, True) + landing(3 * n1, True) + landing(n1)
        + [pltpu.VMEM((4, 16, width), F32), pltpu.VMEM((6, 16, width), F32)]
        + [dma((5, 8)), dma((5, 8)), dma((2,)), dma((2,)), dma((2,)), dma((6,)), dma((6,)), dma((20,)), dma((16,)), dma((4,))],
        compiler_params=params(2),
        name="last_backward",
    )(
        gains, ng, masked, g4, g1, y0, a3, q3, k3, v3, o3, ol3, r3, e3,
        x, a0, q0, k0, v0, o0, ol0, r0, e0, up, down, weights,
    )
    square, tall_square = sd((part, n1), F32), sd((part, n2), F32)
    small = pl.pallas_call(
        unpack,
        in_specs=[vmem] * 3,
        out_specs=[vmem] * 19,
        out_shape=[tall_square if i in (4, 5, 14, 15) else square for i in range(16)]
        + [sd((6, width), F32)] * 2 + [sd((1, width), F32)],
        name="unpack",
    )(sums2, sums3, vec)
    return (decoded, source_grad, target_grad, *small)


def pair_body(*arguments):
    source, target, cotangent, lengths, timesteps, masked, loss_mask = arguments[:7]
    matrices = [m.T if i in TURNED else m for i, m in enumerate(arguments[7:23])]
    norm_gains, norm_shifts, mask_vector = arguments[23:]
    outs = compute_all(
        lengths, timesteps, norm_gains, norm_shifts, mask_vector, masked, loss_mask, matrices, source, target, cotangent
    )
    grads = [g.T if i in TURNED else g for i, g in enumerate(outs[3:19])]
    return (*outs[:3], *grads, outs[19], outs[20], outs[21][0])


def solution(mesh):
    whole_pairs = dict(mesh.shape) == {"dp": 16, "tensor": 2}
    return jax.shard_map(
        pair_body if whole_pairs else body,
        mesh=mesh,
        in_specs=(
            P("dp", "tensor", None),
            P("dp", "tensor", None),
            P("dp", "tensor", None),
            P("dp"),
            P("dp"),
            P("dp", "tensor"),
            P("dp", "tensor"),
            P("dp", "tensor"),
            P("dp", "tensor"),
            P("dp", "tensor"),
            P("tensor", "dp"),
            P("dp", "tensor"),
            P("tensor", "dp"),
            P("dp", "tensor"),
            P("dp", "tensor"),
            P("dp", "tensor"),
            P("tensor", "dp"),
            P("dp", "tensor"),
            P("dp", "tensor"),
            P("dp", "tensor"),
            P("tensor", "dp"),
            P("dp", "tensor"),
            P("tensor", "dp"),
            P(),
            P(),
            P(),
        ),
        out_specs=(
            P("dp", "tensor", None),
            P("dp", "tensor", None),
            P("dp", "tensor", None),
            P("dp", "tensor"),
            P("dp", "tensor"),
            P("dp", "tensor"),
            P("tensor", "dp"),
            P("dp", "tensor"),
            P("tensor", "dp"),
            P("dp", "tensor"),
            P("dp", "tensor"),
            P("dp", "tensor"),
            P("tensor", "dp"),
            P("dp", "tensor"),
            P("dp", "tensor"),
            P("dp", "tensor"),
            P("tensor", "dp"),
            P("dp", "tensor"),
            P("tensor", "dp"),
            P(),
            P(),
            P(),
        ),
        check_vma=False,
    )
```

profile of v0, /device:TPU:0, one launch (start us, length us, event | category | flops | bytes accessed | tf_op | source)
XLA Modules:
  0.0 273.3 jit_solution(4166437995787815330)
XLA Ops:
  0.7 116.5 %forward.1 = (bf16[2,4,2,2,32,7168]{5,4,3,2,1,0:T(8,128)(2,1)}, bf16[1024,512]{1,0:T(8,128)(2,1)}, bf16[1024,512]{1,0:T(8,128)(2,1)}, bf16[1024,512]{1,0:T(8,128...) custom-call(s32[2]{0:T(128)} %lengths.1, ...), custom_call_target="tpu_custom_call" | custom-call | tf_op jit(solution)/shard_map/forward/pallas_call | solution.py:1566
  117.2 70.0 %dec_backward.1 = (bf16[2,512,512]{2,1,0:T(8,128)(2,1)}, f32[1024,512]{1,0:T(8,128)}, f32[1024,512]{1,0:T(8,128)}, bf16[2,4,2,2,32,1024]{5,4,3,2,1,0:T(8,128)(2,...) custom-call(f32[6,512]{1,0:T(8,128)} %gains.5, f32[6,512]{1,0:T(8,128)} %shifts.3, ...), custom_call_target="tpu_custom_call" | custom-call | tf_op jit(solution)/shard_map/dec_backward/pallas_call | solution.py:1582
  187.2 78.2 %last_backward.1 = (bf16[2,512,512]{2,1,0:T(8,128)(2,1)}, bf16[2,512,512]{2,1,0:T(8,128)(2,1)}, f32[32,4096]{1,0:T(8,128)}, f32[16,512]{1,0:T(8,128)}) custom-call(f32[6,512]{1,0:T(8,128)} %gains.5, f32[16,512]{1,0:T(8,128)} %get-tuple-element.107.ng2, s32[2,512]{1,0:T(2,128)} %masked.3, f32[1024,512]{1,0:T(8,128)} %get-tuple-element.108.g4_hbm, ...), custom_call_target="tpu_custom_call" | custom-call | tf_op jit(solution)/shard_map/last_backward/pallas_call | solution.py:1596
  265.4 0.0 copy-start
  265.4 2.2 unpack.1
  267.6 2.3 copy.51
  269.9 2.3 copy.52
  272.2 0.0 copy-done
  272.2 1.0 copy.53
Async XLA Ops:
  265.4 6.7 %copy-start = (bf16[2,512,512]{2,1,0:T(8,128)(2,1)S(1)}, bf16[2,512,512]{2,1,0:T(8,128)(2,1)}, u32[]{:S(2)}) copy-start(bf16[2,512,512]{2,1,0:T(8,128)(2,1)} %get-tuple-element.178) | copy-start | bytes 3145732
where the time goes:
time: 278 us; the launch traced here: 273 us
  Pallas kernels  267 us (96%)
  local copies, waits for them, and re-layouts  5.5 us (2%)
    pallas_call x1, Pallas kernels, compute_all(): pl.pallas_call(forward, in_specs=[smem, smem] + [vmem] * 21 + [any_spec]...  117 us
    pallas_call x1, Pallas kernels, compute_all(): pl.pallas_call(last_backward, in_specs=[vmem] * 3 + [any_spec] * 23, out_...  78.2 us
    pallas_call x1, Pallas kernels, compute_all(): pl.pallas_call(dec_backward, in_specs=[vmem, vmem] + [any_spec] * 18, out...  70 us

commit v1 on v0

--- a/solution.py
+++ b/solution.py
@@ -1503,7 +1503,9 @@
     reduce.finish()
 
 
-def unpack(sums2, sums3, vec, *refs):
+def unpack(dec, sg, tg, sums2, sums3, vec, dec_o, sg_o, tg_o, *refs):
+    for src, dst in ((dec, dec_o), (sg, sg_o), (tg, tg_o)):
+        dst[...] = src[...]
     grads, (gains_o, shifts_o, mask_o) = refs[:16], refs[16:]
     for summed, held in ((sums2, (14, 15, 10, 11, 12, 13)), (sums3, (4, 5, 6, 7, 8, 9, 0, 1, 2, 3))):
         offset = 0
@@ -1613,13 +1615,14 @@
     square, tall_square = sd((part, n1), F32), sd((part, n2), F32)
     small = pl.pallas_call(
         unpack,
-        in_specs=[vmem] * 3,
-        out_specs=[vmem] * 19,
-        out_shape=[tall_square if i in (4, 5, 14, 15) else square for i in range(16)]
+        in_specs=[vmem] * 6,
+        out_specs=[vmem] * 22,
+        out_shape=[halves] * 3 + [tall_square if i in (4, 5, 14, 15) else square for i in range(16)]
         + [sd((6, width), F32)] * 2 + [sd((1, width), F32)],
+        compiler_params=pltpu.CompilerParams(vmem_limit_bytes=VMEM_LIMIT),
         name="unpack",
-    )(sums2, sums3, vec)
-    return (decoded, source_grad, target_grad, *small)
+    )(decoded, source_grad, target_grad, sums2, sums3, vec)
+    return tuple(small)
 
 
 def pair_body(*arguments):

time: 278 us -> 274 us (0.986)
  local copies, waits for them, and re-layouts: 5.5 us -> 0 us
    unnamed x5 -> x0, local copies, waits for them, and re-layouts: 5.5 us -> none
where the time goes in v1:
time: 274 us; the launch traced here: 270 us
  Pallas kernels  269 us (98%)
    pallas_call x1, Pallas kernels, compute_all(): pl.pallas_call(forward, in_specs=[smem, smem] + [vmem] * 21 + [any_spec]...  117 us
    pallas_call x1, Pallas kernels, compute_all(): pl.pallas_call(last_backward, in_specs=[vmem] * 3 + [any_spec] * 23, out_...  78.2 us
    pallas_call x1, Pallas kernels, compute_all(): pl.pallas_call(dec_backward, in_specs=[vmem, vmem] + [any_spec] * 18, out...  70 us

profile of v1, /device:TPU:0, one launch (start us, length us, event | category | flops | bytes accessed | tf_op | source)
XLA Modules:
  0.0 269.8 jit_solution(8066910950288137347)
XLA Ops:
  0.7 116.5 %forward.1 = (bf16[2,4,2,2,32,7168]{5,4,3,2,1,0:T(8,128)(2,1)}, bf16[1024,512]{1,0:T(8,128)(2,1)}, bf16[1024,512]{1,0:T(8,128)(2,1)}, bf16[1024,512]{1,0:T(8,128...) custom-call(s32[2]{0:T(128)} %lengths.1, ...), custom_call_target="tpu_custom_call" | custom-call | tf_op jit(solution)/shard_map/forward/pallas_call | solution.py:1568
  117.2 70.0 %dec_backward.1 = (bf16[2,512,512]{2,1,0:T(8,128)(2,1)}, f32[1024,512]{1,0:T(8,128)}, f32[1024,512]{1,0:T(8,128)}, bf16[2,4,2,2,32,1024]{5,4,3,2,1,0:T(8,128)(2,...) custom-call(f32[6,512]{1,0:T(8,128)} %gains.5, f32[6,512]{1,0:T(8,128)} %shifts.3, ...), custom_call_target="tpu_custom_call" | custom-call | tf_op jit(solution)/shard_map/dec_backward/pallas_call | solution.py:1584
  187.2 78.2 %last_backward.1 = (bf16[2,512,512]{2,1,0:T(8,128)(2,1)}, bf16[2,512,512]{2,1,0:T(8,128)(2,1)}, f32[32,4096]{1,0:T(8,128)}, f32[16,512]{1,0:T(8,128)}) custom-call(f32[6,512]{1,0:T(8,128)} %gains.5, f32[16,512]{1,0:T(8,128)} %get-tuple-element.110.ng2, s32[2,512]{1,0:T(2,128)} %masked.3, f32[1024,512]{1,0:T(8,128)} %get-tuple-element.111.g4_hbm, ...), custom_call_target="tpu_custom_call" | custom-call | tf_op jit(solution)/shard_map/last_backward/pallas_call | solution.py:1598
  265.4 4.2 %unpack.1 = (bf16[2,512,512]{2,1,0:T(8,128)(2,1)}, bf16[2,512,512]{2,1,0:T(8,128)(2,1)}, bf16[2,512,512]{2,1,0:T(8,128)(2,1)}, f32[32,256]{1,0:T(8,128)}, f32[32...) custom-call(bf16[2,512,512]{2,1,0:T(8,128)(2,1)} %get-tuple-element., ...), custom_call_target="tpu_custom_call" | custom-call | tf_op jit(solution)/shard_map/unpack/pallas_call | solution.py:1616
